TPU v7x, 128 devices: a whole 4x4x4 slice. The times are simulated.
128 devices in a mesh: replica: 16 (over z, x_lo, core), mp: 8 (over x_hi, y).
Axes of the slice: x: 4 (x_hi: 2, x_lo: 2; x = x_hi * 2 + x_lo), y: 4, z: 4, core: 2. Of those that a mesh axis runs over, the one named last changes fastest.
Arguments:
- hidden: bfloat16 [8192, 7168], P('replica', 'mp'), may hold values from -6 to 6
- inner_down: bfloat16 [16, 7168, 4096], P('replica', 'mp'), may hold values from -6 to 6
- residual_in: bfloat16 [8192, 4096], P(('replica', 'mp')), may hold values from -120 to 120
- gain: float32 [4096], replicated, may hold values from 0.25 to 1.75
- cotangent: bfloat16 [8192, 4096], P(('replica', 'mp')), may hold values from -6 to 6
- codes: bfloat16 [16, 4096, 4096], P('replica', 'mp'), may hold values from -448 to 448, as said below
- scales: float32 [16, 4096, 32], P('replica', 'mp'), may hold values from 0.005 to 0.06
- outer_params: float32 [4096, 4096], P('mp', 'replica'), may hold values from -6 to 6
- momentum: float32 [4096, 4096], P('mp', 'replica'), may hold values from -1.8 to 1.8
Outputs:
- normed: bfloat16 [8192, 4096], P(('replica', 'mp'))
- grad_hidden: bfloat16 [8192, 7168], P('replica', 'mp')
- grad_gain: float32 [16, 4096], P('replica')
- new_params: float32 [4096, 4096], P('mp', 'replica')
- new_momentum: float32 [4096, 4096], P('mp', 'replica')
- merged: bfloat16 [16, 4096, 4096], P('replica', 'mp')
Inputs may be any that keep to these rules, and one draw needn't show every extreme that they name: `codes`: every entry is a value of the e4m3 eight-bit float format (three mantissa bits), at most 448 in magnitude.
All inputs are finite; a program needn't handle non-finite values.
Results may differ from a plain program's by a relative error of at most 0.022.
Values may be sent and summed in bfloat16 or wider, within the bound.
A program may use at most 128 MiB of HBM per device.

v0:
```python
import jax
import jax.numpy as jnp
from jax import lax
from jax.sharding import PartitionSpec as P

FF = 7168
BLOCK = 128


momentum_rate = 0.9
outer_rate = 0.7
mix_rate = 0.5


def normalize(resid_rows, summed):
    mixed = resid_rows.astype(jnp.float32) + summed
    inv_rms = lax.rsqrt(jnp.mean(mixed * mixed, -1, keepdims=True) + 1e-05)
    return (mixed * inv_rms, inv_rms)


def backward(cot_rows, unit_rows, inv_rms, gain):
    scaled = cot_rows.astype(jnp.float32) * gain
    grad_mixed = inv_rms * (scaled - unit_rows * jnp.mean(scaled * unit_rows, -1, keepdims=True))
    return grad_mixed.astype(jnp.bfloat16)


def project_back(grad_rows, weights):
    product = lax.dot_general(
        grad_rows, weights, (((1,), (1,)), ((), ())), preferred_element_type=jnp.float32
    )
    return (product * FF ** (-0.5)).astype(jnp.bfloat16)


def decode(code_block, scale_block):
    layout = code_block.shape
    widened = code_block.astype(jnp.float32).reshape(layout[:-1] + (layout[-1] // BLOCK, BLOCK))
    return (widened * scale_block[..., None]).reshape(layout)


def shards(hidden, inner_down, residual_in, gain, cotangent, codes, scales, outer_params, momentum):
    weights = inner_down[0]
    scale_ff = FF ** (-0.5)
    own_rows = residual_in.shape[0]
    partial_value = jnp.dot(hidden, weights, preferred_element_type=jnp.float32) * scale_ff
    summed = lax.psum(partial_value.astype(jnp.bfloat16), "mp").astype(jnp.float32)
    resid_all, cot_all = (
        lax.all_gather(residual_in, "mp", axis=0, tiled=True),
        lax.all_gather(cotangent, "mp", axis=0, tiled=True),
    )
    unit_rows, inv_rms = normalize(resid_all, summed)
    grad_gain = jnp.sum(cot_all.astype(jnp.float32) * unit_rows, 0)
    row_start = lax.axis_index("mp") * own_rows
    own_unit = lax.dynamic_slice_in_dim(unit_rows, row_start, own_rows, 0)
    normed = (own_unit * gain).astype(jnp.bfloat16)
    grad_mixed = backward(cot_all, unit_rows, inv_rms, gain)
    grad_hidden = project_back(grad_mixed, weights)
    replica_count = lax.axis_size("replica")
    share_width = codes.shape[2] // replica_count
    summed_all = lax.psum(decode(codes[0], scales[0]).astype(jnp.bfloat16), "replica").astype(
        jnp.float32
    )
    own_sum = lax.dynamic_slice_in_dim(
        summed_all, lax.axis_index("replica") * share_width, share_width, 1
    )
    outer_step = own_sum / replica_count
    new_momentum = momentum_rate * momentum + outer_step
    new_params = outer_params - outer_rate * (outer_step + momentum_rate * new_momentum)
    fresh = new_params.astype(jnp.bfloat16)
    full_rows = lax.all_gather(fresh, "replica", axis=1, tiled=True)
    inner_fragment = weights[: codes.shape[1]]
    merged = (
        mix_rate * inner_fragment.astype(jnp.float32)
        + (1.0 - mix_rate) * full_rows.astype(jnp.float32)
    ).astype(jnp.bfloat16)
    return (normed, grad_hidden, grad_gain[None], new_params, new_momentum, merged[None])


def solution(mesh):
    placed = (
        P("replica", "mp"),
        P("replica", "mp", None),
        P(("replica", "mp"), None),
        P(),
        P(("replica", "mp"), None),
        P("replica", "mp", None),
        P("replica", "mp", None),
        P("mp", "replica"),
        P("mp", "replica"),
    )
    return jax.shard_map(
        shards,
        mesh=mesh,
        in_specs=placed,
        out_specs=(
            P(("replica", "mp"), None),
            P("replica", "mp"),
            P("replica", None),
            P("mp", "replica"),
            P("mp", "replica"),
            P("replica", "mp", None),
        ),
        check_vma=False,
    )
```

profile of v0, /device:TPU:1, one launch (start us, length us, event | category | flops | bytes accessed | tf_op | source)
XLA Modules:
  0.0 472.6 jit_solution(10604813328665545955)
XLA Ops:
  7.2 0.0 copy-start
  7.2 0.0 all-reduce.5.cloned.1.call-start
  7.2 1.0 copy.15
  8.3 0.0 copy-start.2
  8.3 2.3 mul.112
  10.6 0.0 copy-done.2
  10.6 7.1 %fusion.6 = bf16[512,4096]{1,0:T(8,128)(2,1)} fusion(f32[64,8,32,128]{3,2,1,0:T(8,128)S(1)} %bitcast.25, bf16[1,512,4096]{2,1,0:T(8,128)(2,1)S(1)} %copy-done.2), kind=kLoop, calls=%fused_computation.9 | loop fusion | flops 6291456 | bytes 16777216 | tf_op jit(solution)/shard_map/convert_element_type | solution.py:59
  17.7 0.0 all-reduce.5.cloned.1.call-update
  17.8 0.0 copy-start.4
  17.8 0.0 copy-start.5
  17.8 0.0 all-reduce.3.cloned.1.call-start
  17.8 0.0 copy-done
  17.8 9.3 %multiply_convert_fusion = bf16[512,4096]{1,0:T(8,128)(2,1)} fusion(bf16[512,896]{1,0:T(8,128)(2,1)S(1)} %copy-done, bf16[1,896,4096]{2,1,0:T(8,128)(2,1)} %param.10), kind=kOutput, calls=%fused_computation.15 | convolution fusion | flops 3762290688 | bytes 12451840 | tf_op jit(solution)/shard_map/dot_general | solution.py:44
  27.1 0.0 all-reduce.3.cloned.1.call-update
  27.1 0.0 all-gather.4.cloned.1.call-start
  27.2 0.7 all-gather.4.cloned.1.call-update
  27.9 0.0 all-gather.6.cloned.1.call-start
  27.9 0.5 all-gather.6.cloned.1.call-update
  28.4 0.2 all-gather.8.cloned.1.call-start
  28.7 127.2 %all-reduce.5.cloned.1.call-done = bf16[512,4096]{1,0:T(8,128)(2,1)} async-done(((bf16[512,4096]{1,0:T(8,128)(2,1)}), bf16[512,4096]{1,0:T(8,128)(2,1)}) %all-reduce.5.cloned.1.call-update) | async-done | bytes 4194320 | tf_op jit(solution)/shard_map/psum | solution.py:59
  155.9 2.1 fusion.25
  158.0 0.0 all-gather.8.cloned.1.call-update
  158.1 111.7 %all-reduce.3.cloned.1.call-done = bf16[512,4096]{1,0:T(8,128)(2,1)} async-done(((bf16[512,4096]{1,0:T(8,128)(2,1)}), bf16[512,4096]{1,0:T(8,128)(2,1)}) %all-reduce.3.cloned.1.call-update) | async-done | bytes 4194320 | tf_op jit(solution)/shard_map/psum | solution.py:45
  269.8 72.0 %all-gather.4.cloned.1.call-done = bf16[512,4096]{1,0:T(8,128)(2,1)} async-done(((bf16[64,4096]{1,0:T(8,128)(2,1)}), bf16[512,4096]{1,0:T(8,128)(2,1)}) %all-gather.4.cloned.1.call-update) | async-done | bytes 4194320 | tf_op jit(solution)/shard_map/all_gather | solution.py:47
  341.7 4.9 %multiply_reduce_fusion = f32[512]{0:T(512)S(1)} fusion(bf16[512,4096]{1,0:T(8,128)(2,1)} %all-reduce.3.cloned.1.call-done, bf16[512,4096]{1,0:T(8,128)(2,1)} %all-gather.4.cloned.1.call-done), kind=kLoop, calls=%fused_computation.13 | loop fusion | flops 10485248 | bytes 8390656 | tf_op jit(solution)/shard_map/reduce_sum | solution.py:17
  346.6 66.5 %all-gather.6.cloned.1.call-done = bf16[512,4096]{1,0:T(8,128)(2,1)} async-done(((bf16[64,4096]{1,0:T(8,128)(2,1)}), bf16[512,4096]{1,0:T(8,128)(2,1)}) %all-gather.6.cloned.1.call-update) | async-done | bytes 4194320 | tf_op jit(solution)/shard_map/all_gather | solution.py:48
  413.2 8.5 %fusion.5 = (f32[4096]{0:T(1024)}, f32[512]{0:T(512)S(1)}, f32[512,4096]{1,0:T(8,128)S(1)}) fusion(bf16[512,4096]{1,0:T(8,128)(2,1)} %all-gather.6.cloned.1.call-done, f32[4096]{0:T(1024)S(1)} %copy-done.6, f32[512]{0:T(512)S(1)} %add_rsqrt_fusion, bf16[512,4096]{1,0:T(8,128)(2,1)} %all-reduce.3.cloned.1.call-done, ...), kind=kLoop, calls=%fused_computation.7 | loop fusion | flops 20966912 | bytes 21008384 | tf_op jit(solution)/shard_map/reduce_sum | solution.py:51
  421.7 0.9 multiply_convert_fusion.2
  422.5 8.7 %multiply_convert_fusion.1 = bf16[512,896]{1,0:T(8,128)(2,1)} fusion(bf16[1,896,4096]{2,1,0:T(8,128)(2,1)} %param.10, bf16[512,4096]{1,0:T(8,128)(2,1)S(1)} %copy-done.3, f32[512,4096]{1,0:T(8,128)S(1)} %get-tuple-element.11, f32[512]{0:T(512)S(1)} %broadcast_multiply_fusion, f32[4096]{0:T(1024)S(1)} %copy-done.6, f32[512]{0:T(512)S(1)} %add_rsqrt_fusion), kind=kOutput, calls=%fused_computation.25 | convolution fusion | flops 3771596800 | bytes 20860928 | tf_op jit(solution)/shard_map/dot_general | solution.py:28
  431.2 27.7 %all-gather.8.cloned.1.call-done = bf16[512,4096]{1,0:T(8,128)(2,1)} async-done(((bf16[512,256]{1,0:T(8,128)(2,1)}), bf16[512,4096]{1,0:T(8,128)(2,1)}) %all-gather.8.cloned.1.call-update) | async-done | bytes 4194320 | tf_op jit(solution)/shard_map/all_gather | solution.py:69
  458.9 7.2 %fusion.16 = bf16[1,512,4096]{2,1,0:T(8,128)(2,1)} fusion(bf16[512,4096]{1,0:T(8,128)(2,1)} %all-gather.8.cloned.1.call-done, bf16[1,896,4096]{2,1,0:T(8,128)(2,1)} %param.10), kind=kLoop, calls=%fused_computation.21 | loop fusion | flops 10485760 | bytes 12582912 | tf_op jit(solution)/shard_map/broadcast_in_dim | solution.py:75
  466.1 0.0 copy-done.1
  (9 shorter events, 0.0 us)
Async XLA Ops:
  7.2 10.7 %copy-start = (bf16[512,896]{1,0:T(8,128)(2,1)S(1)}, bf16[512,896]{1,0:T(8,128)(2,1)}, u32[]{:S(2)}) copy-start(bf16[512,896]{1,0:T(8,128)(2,1)} %param.9) | copy-start | bytes 2752516
  7.2 148.7 %all-reduce.5.cloned.1.call-start = ((), (), s32[]{:S(2)}) async-start(), calls=%async_computation.3 | async-start | bytes 8388608 | tf_op jit(solution)/shard_map/psum | solution.py:59
  8.3 2.3 copy-start.2
  17.8 138.1 %copy-start.4 = (f32[512,256]{1,0:T(8,128)S(1)}, f32[512,256]{1,0:T(8,128)}, u32[]{:S(2)}) copy-start(f32[512,256]{1,0:T(8,128)} %param.16) | copy-start | bytes 1572868
  17.8 138.1 %copy-start.5 = (f32[512,256]{1,0:T(8,128)S(1)}, f32[512,256]{1,0:T(8,128)}, u32[]{:S(2)}) copy-start(f32[512,256]{1,0:T(8,128)} %param.17) | copy-start | bytes 1572868
  17.8 252.0 %all-reduce.3.cloned.1.call-start = ((), (), s32[]{:S(2)}) async-start(), calls=%async_computation.1 | async-start | bytes 8388608 | tf_op jit(solution)/shard_map/psum | solution.py:45
  27.1 386.0 %copy-start.6 = (f32[4096]{0:T(1024)S(1)}, f32[4096]{0:T(1024)}, u32[]{:S(2)}) copy-start(f32[4096]{0:T(1024)} %param.12) | copy-start | bytes 49156
  27.1 314.6 %all-gather.4.cloned.1.call-start = ((), (), s32[]{:S(2)}) async-start(), calls=%async_computation | async-start | bytes 4718592 | tf_op jit(solution)/shard_map/all_gather | solution.py:47
  27.9 385.3 %all-gather.6.cloned.1.call-start = ((), (), s32[]{:S(2)}) async-start(), calls=%async_computation.2 | async-start | bytes 4718592 | tf_op jit(solution)/shard_map/all_gather | solution.py:48
  28.4 430.4 %all-gather.8.cloned.1.call-start = ((), (), s32[]{:S(2)}) async-start(), calls=%async_computation.4 | async-start | bytes 4456448 | tf_op jit(solution)/shard_map/all_gather | solution.py:69
  413.2 9.4 %copy-start.3 = (bf16[512,4096]{1,0:T(8,128)(2,1)S(1)}, bf16[512,4096]{1,0:T(8,128)(2,1)}, u32[]{:S(2)}) copy-start(bf16[512,4096]{1,0:T(8,128)(2,1)} %all-gather.6.cloned.1.call-done) | copy-start | bytes 12582916
  422.5 43.6 %copy-start.1 = (bf16[512,896]{1,0:T(8,128)(2,1)S(1)}, bf16[512,896]{1,0:T(8,128)(2,1)}, u32[]{:S(2)}) copy-start(bf16[512,896]{1,0:T(8,128)(2,1)} %param.9) | copy-start | bytes 2752516
Sparse Core Ops, SparseCore 0:
  17.9 137.9 all-reduce.4
  159.0 110.7 all-reduce.2
  272.1 69.5 all-gather.3
  343.9 69.1 all-gather.5
  414.6 44.2 all-gather.7
where the time goes:
time: 473 us
  waiting for transfers between devices  406 us (86%)
  other arithmetic  30.8 us (7%)
  matrix products  17.9 us (4%)
  between operations  13.9 us (3%)
    psum x1, waiting for transfers between devices, shards(): lax.psum(decode(codes[0], scales[0]).astype(jnp.bfloat16), 'replica')  127 us
    psum x1, waiting for transfers between devices, shards(): lax.psum(partial_value.astype(jnp.bfloat16), 'mp').astype(jnp.float32)  112 us
    all_gather x1, waiting for transfers between devices, shards(): lax.all_gather(residual_in, 'mp', axis=0, tiled=True)  72 us
    all_gather x1, waiting for transfers between devices, shards(): lax.all_gather(cotangent, 'mp', axis=0, tiled=True)  66.5 us
    all_gather x1, waiting for transfers between devices, shards(): full_rows = lax.all_gather(fresh, 'replica', axis=1, tiled=True)  27.7 us
  transfers between devices with their start and end apart: 5, of which 5 were waited for; matrix products, arithmetic and copies ran while one was open for 7% of the time, Pallas kernels for 0%

commit v1 on v0

v1 whole, which is shorter than its diff:
```python
import functools

import jax
import jax.numpy as jnp
from jax import lax
from jax.experimental import pallas as pl
from jax.experimental.pallas import tpu as pltpu
from jax.sharding import PartitionSpec as P

FF = 7168
BLOCK = 128
MESH = pl.DeviceIdType.MESH

momentum_rate = 0.9
outer_rate = 0.7
mix_rate = 0.5

D = 4096
UNITS = 896
ROWS = 16
CHUNKS = 4
PARTS = 2
FRAG_ROWS = 512
PART = FRAG_ROWS // PARTS
SHARE = 256
HALF = D // 2
X_FIRST = (False, True, False, False)
CUT = 512
PLACE_ROWS = 128
N_SEND, N_RECV, N_LOCAL = 160, 160, 40

SCHEDULE = (
    ("mm1", 0), ("dec", 0), ("mm1", 1), ("mm1", 2), ("zs", 0), ("mid", 0), ("mm1", 3), ("dec", 1),
    ("zm", 0), ("zs", 1), ("mid", 2), ("ze", 0), ("xadd", 1), ("end", 0), ("zm", 1), ("mid", 3),
    ("up", 0), ("ze", 1), ("norm", 0), ("end", 2), ("mid", 1), ("bp", 0), ("up", 1), ("end", 3),
    ("bf", 0), ("agp", 0), ("end", 1), ("norm", 1), ("norm", 2), ("agf", 0), ("bc", 0), ("bp", 1),
    ("mg", 0), ("norm", 3), ("gg", 0), ("agf", 1), ("bf", 1), ("agx", 0), ("agp", 2), ("gg", 1),
    ("mm2", 0), ("bc", 1), ("agp", 3), ("agx", 1), ("mm3", 0), ("gg", 2), ("mg", 1), ("agf", 2),
    ("agf", 3), ("mm2", 1), ("agx", 2), ("gg", 3), ("mm2", 2), ("mm3", 1), ("agx", 3), ("mm2", 3),
    ("mm3", 3), ("mm3", 2),
)


class Ring:
    def __init__(self, kit, pos, nxt, prv):
        self.kit, self.pos, self.nxt, self.prv = kit, pos, nxt, prv

    def at(self, step):
        return lax.rem(self.pos + (step % 4), 4)

    def scatter(self, piece, fwd, own, total):
        kit = self.kit
        self.piece, self.fwd, self.own, self.total = piece, fwd, own, total
        two = self.at(2)
        self.got_fwd = (
            kit.send(piece(two, 0), fwd(0), self.nxt),
            kit.send(piece(two, 1), fwd(1), self.prv),
        )
        got_right = kit.send(piece(self.at(1), 1), own(1), self.nxt)
        got_left = kit.send(piece(self.at(3), 0), own(0), self.prv)
        self.got_own = (got_left, got_right)

    def middle(self):
        kit, out = self.kit, []
        for k, (step, to) in enumerate(((1, self.nxt), (3, self.prv))):
            self.got_fwd[k].wait_recv()
            mine = self.piece(self.at(step), k)
            add_into(mine, self.fwd(k))
            out.append(kit.send(mine, self.total(k), to))
        self.got_total = out

    def finish(self):
        for k in range(2):
            self.got_own[k].wait_recv()
            self.got_total[k].wait_recv()

    def gather_open(self, slot):
        self.slot = slot
        self.base = [self.kit.recv_slots(2), self.kit.recv_slots(2)]

    def gather(self, k):
        kit, mine = self.kit, self.slot(self.pos, k)
        kit.send(mine, mine, self.nxt, self.base[0] + k)
        kit.send(mine, mine, self.prv, self.base[1] + k)

    def await_near(self, way, k):
        there = self.slot(self.at(3 if way == 0 else 1), k)
        self.kit.wait_on(there, self.base[way] + k)

    def forward(self):
        kit = self.kit
        self.far = []
        for k, (step, to) in enumerate(((3, self.nxt), (1, self.prv))):
            self.await_near(k, k)
            there = self.slot(self.at(step), k)
            index = kit.recv_slots(1)
            kit.send(there, there, to, index)
            self.far.append(index)

    def await_rest(self):
        self.await_near(0, 1)
        self.await_near(1, 0)

    def await_far(self):
        for k in range(2):
            self.kit.wait_on(self.slot(self.at(2), k), self.far[k])


class Kit:
    def __init__(self, ssem, rsem, lsem):
        self.ssem, self.rsem, self.lsem = ssem, rsem, lsem
        self.sends, self.recvs, self.locals = 0, 0, 0
        self.open = []

    def recv_slots(self, n):
        self.recvs += n
        assert self.recvs <= N_RECV
        return self.recvs - n

    def send(self, src, dst, to, index=None):
        if index is None:
            index = self.recv_slots(1)
        copy = pltpu.make_async_remote_copy(
            src_ref=src,
            dst_ref=dst,
            send_sem=self.ssem.at[self.sends],
            recv_sem=self.rsem.at[index],
            device_id=to,
            device_id_type=MESH,
        )
        self.sends += 1
        assert self.sends <= N_SEND
        copy.start()
        self.open.append(copy.wait_send)
        return copy

    def wait_on(self, ref, index):
        pltpu.make_async_copy(ref, ref, self.rsem.at[index]).wait()

    def local(self, src, dst):
        copy = pltpu.make_async_copy(src, dst, self.lsem.at[self.locals])
        self.locals += 1
        assert self.locals <= N_LOCAL
        copy.start()
        return copy

    def out(self, src, dst):
        self.open.append(self.local(src, dst).wait)


def f32(value):
    return value.astype(jnp.float32)


def add_into(a, b):
    a[...] = (f32(a[...]) + f32(b[...])).astype(jnp.bfloat16)


def sync_kernel(
    hidden, weights, resid, gain, cot, codes, scales, params, mom,
    normed_o, hgrad_o, ggain_o, params_o, mom_o, merged_o,
    w, hid, lhs, prod, a_fwd, a_own, a_sum, a_x, a_x4, gm, res, ct, gn, mixed, nrm, hg, gg, gs, gr,
    cd, sc, dec, core_in, b_fwd, b_own, b_sum, b_x, fresh, pr, mo,
    ssem, rsem, lsem,
):
    kit = Kit(ssem, rsem, lsem)
    r, m = lax.axis_index("replica"), lax.axis_index("mp")
    z, xl, c = r // 4, lax.rem(r // 2, 2), lax.rem(r, 2)
    xh, y = m // 4, lax.rem(m, 4)

    def place(z, xl, c, xh, y):
        return (z * 4 + xl * 2 + c, xh * 4 + y)

    y_next, y_prev = place(z, xl, c, xh, lax.rem(y + 1, 4)), place(z, xl, c, xh, lax.rem(y + 3, 4))
    z_next, z_prev = place(lax.rem(z + 1, 4), xl, c, xh, y), place(lax.rem(z + 3, 4), xl, c, xh, y)
    x_far, x_near, other = place(z, xl, c, 1 - xh, y), place(z, 1 - xl, c, xh, y), place(z, xl, 1 - c, xh, y)

    load_hid = kit.local(hidden, hid)
    width = D // 4
    load_w = [
        kit.local(weights.at[:, pl.ds(i * width, width)], w.at[:, pl.ds(i * width, width)])
        for i in range(4)
    ]
    loads = {}

    def load_rest():
        loads["sc"] = kit.local(scales, sc)
        for i in range(PARTS):
            rows = pl.ds(i * PART, PART)
            loads["cd", i] = kit.local(codes.at[rows], cd.at[rows])
        loads["norm"] = [kit.local(resid, res), kit.local(cot, ct), kit.local(gain, gn)]
        loads["outer"] = [kit.local(params, pr), kit.local(mom, mo)]

    barrier = pltpu.get_barrier_semaphore()
    peers = (y_next, y_prev, z_next, z_prev, x_far, x_near, other)
    for peer in peers:
        pl.semaphore_signal(barrier, inc=1, device_id=peer, device_id_type=MESH)

    scale_ff = FF ** (-0.5)
    ring_a = [Ring(kit, y, y_next, y_prev) for _ in range(CHUNKS)]
    ring_b = [Ring(kit, z, z_next, z_prev) for _ in range(PARTS)]
    state = {}
    load_hid.wait()

    def half(k):
        return pl.ds(k * HALF, HALF)

    def ring_start(i):
        if X_FIRST[i]:
            ring_a[i].scatter(
                lambda pos, k: prod.at[i, pos, xh, :, half(k)],
                lambda k: a_fwd.at[i, 0, :, half(k)],
                lambda k: a_own.at[i, 0, :, half(k)],
                lambda k: a_sum.at[i, 0, :, half(k)],
            )
        else:
            ring_a[i].scatter(
                lambda pos, k: prod.at[i, pos, k],
                lambda k: a_fwd.at[i, k],
                lambda k: a_own.at[i, k],
                lambda k: a_sum.at[i, k],
            )

    def mm1(i):
        for yy in range(4):
            for xx in range(2):
                lhs[pl.ds((yy * 2 + xx) * ROWS, ROWS), :] = hid[
                    pl.ds((xx * 4 + yy) * 64 + i * ROWS, ROWS), :
                ]
        for q in range(4):
            if i == 0:
                load_w[q].wait()
            cols = pl.ds(q * width, width)
            out = jnp.dot(lhs[...], w[:, cols], preferred_element_type=jnp.float32)
            out = (out * scale_ff).astype(jnp.bfloat16)
            prod[i, :, :, :, cols] = out.reshape(4, 2, ROWS, width)
        if i == 0:
            load_rest()
            pl.semaphore_wait(barrier, len(peers))

        if X_FIRST[i]:
            state["x4", i] = kit.send(prod.at[i, :, 1 - xh], a_x4, x_far)
        else:
            ring_start(i)

    def xadd(i):
        if not X_FIRST[i]:
            return
        state["x4", i].wait_recv()
        for pos in range(4):
            add_into(prod.at[i, pos, xh], a_x4.at[pos])
        ring_start(i)

    def mid(i):
        ring_a[i].middle()

    def end(i):
        ring_a[i].finish()
        if X_FIRST[i]:
            return
        k = 1 - xh
        gone = prod.at[i, y, k]
        gone[...] = (f32(gone[...]) + f32(a_own[i, k]) + f32(a_sum[i, k])).astype(jnp.bfloat16)
        state["x", i] = kit.send(gone, a_x.at[i], x_far)

    def norm(i):
        if i == 0:
            for load in loads["norm"]:
                load.wait()
        if not X_FIRST[i]:
            state["x", i].wait_recv()
        rows = pl.ds(i * ROWS, ROWS)
        step = D // 4
        square = jnp.zeros((ROWS, 1), jnp.float32)
        for q in range(4):
            cols = pl.ds(q * step, step)
            if X_FIRST[i]:
                terms = (prod[i, y, xh, :, cols], a_own[i, 0, :, cols], a_sum[i, 0, :, cols])
            else:
                terms = (prod[i, y, xh, :, cols], a_own[i, xh, :, cols], a_sum[i, xh, :, cols], a_x[i, :, cols])
            value = f32(res[rows, cols])
            for term in terms:
                value = value + f32(term)
            mixed[:, cols] = value
            square = square + jnp.sum(value * value, -1, keepdims=True)
        inv = lax.rsqrt(square / D + 1e-05)
        along = jnp.zeros((ROWS, 1), jnp.float32)
        for q in range(4):
            cols = pl.ds(q * step, step)
            unit = mixed[:, cols] * inv
            mixed[:, cols] = unit
            gain_row = gn[:, cols]
            nrm[rows, cols] = (unit * gain_row).astype(jnp.bfloat16)
            cot_rows = f32(ct[rows, cols])
            along = along + jnp.sum(cot_rows * gain_row * unit, -1, keepdims=True)
            pair = cot_rows * unit
            pair = pair[:8] + pair[8:]
            if i == 0:
                gg[:, cols] = pair
            else:
                gg[:, cols] += pair
        along = along / D
        for q in range(4):
            cols = pl.ds(q * step, step)
            scaled = f32(ct[rows, cols]) * gn[:, cols]
            gm[i, y, xh, :, cols] = (inv * (scaled - mixed[:, cols] * along)).astype(jnp.bfloat16)
        if X_FIRST[i]:
            ring_a[i].gather_open(lambda pos, k: gm.at[i, pos, xh, :, half(k)])
            ring_a[i].gather(0)
            ring_a[i].gather(1)
            state["gx", i] = kit.recv_slots(4)
            mine = gm.at[i, y, xh]
            kit.send(mine, mine, x_far, state["gx", i] + y)
        else:
            ring_a[i].gather_open(lambda pos, k: gm.at[i, pos, k])
            mine = gm.at[i, y, xh]
            state["gx", i] = kit.recv_slots(1)
            kit.send(mine, mine, x_far, state["gx", i])
            ring_a[i].gather(xh)
        if i == CHUNKS - 1:
            kit.out(nrm, normed_o)

    def agp(i):
        if not X_FIRST[i]:
            kit.wait_on(gm.at[i, y, 1 - xh], state["gx", i])
            ring_a[i].gather(1 - xh)

    def agf(i):
        ring = ring_a[i]
        ring.forward()
        ring.await_rest()
        if X_FIRST[i]:
            for step in (1, 3):
                there = gm.at[i, ring.at(step), xh]
                kit.send(there, there, x_far, state["gx", i] + ring.at(step))

    def agx(i):
        ring = ring_a[i]
        ring.await_far()
        if X_FIRST[i]:
            there = gm.at[i, ring.at(2), xh]
            kit.send(there, there, x_far, state["gx", i] + ring.at(2))

    def back(i, first, count):
        units = pl.ds(first, count)
        out = lax.dot_general(
            w[units, :],
            gm[i].reshape(8 * ROWS, D),
            (((1,), (1,)), ((), ())),
            preferred_element_type=jnp.float32,
        )
        out = (out * scale_ff).T.astype(jnp.bfloat16)
        for yy in range(4):
            for xx in range(2):
                at = (yy * 2 + xx) * ROWS
                hg[pl.ds((xx * 4 + yy) * 64 + i * ROWS, ROWS), units] = out[at : at + ROWS]
        state["hg"] = state.get("hg", 0) + 1
        if state["hg"] == 2 * CHUNKS:
            kit.out(hg, hgrad_o)

    def mm2(i):
        if X_FIRST[i]:
            for pos in range(4):
                kit.wait_on(gm.at[i, pos, 1 - xh], state["gx", i] + pos)
        back(i, 0, CUT)

    def mm3(i):
        back(i, CUT, UNITS - CUT)

    def gain_sum(step):
        partner = (x_far, None, None)[step] if step < 1 else None
        if step == 0:
            gs[0] = jnp.sum(gg[...], 0, keepdims=True)
        elif step < 4:
            state["gg", step - 1].wait_recv()
            gs[step] = gs[step - 1] + gr[step - 1]
        if step == 1:
            partner = place(z, xl, c, xh, y + 1 - 2 * lax.rem(y, 2))
        if step == 2:
            partner = place(z, xl, c, xh, 3 - y)
        if step < 3:
            state["gg", step] = kit.send(gs.at[step], gr.at[step], partner)
        else:
            kit.out(gs.at[3], ggain_o)

    def decode(k):
        if k == 0:
            loads["sc"].wait()
        loads["cd", k].wait()
        rows = pl.ds(k * PART, PART)
        factors = sc[:, rows].T
        for j in range(D // BLOCK):
            target, part = j // 2, j % 2
            value = f32(cd[rows, pl.ds(j * BLOCK, BLOCK)]) * factors[:, j : j + 1]
            dec[k, target % 2, target // 4, (target // 2) % 2, :, pl.ds(part * BLOCK, BLOCK)] = value.astype(
                jnp.bfloat16
            )
        state["core", k] = kit.send(dec.at[k, 1 - c], core_in.at[k], other)

    def zs(k):
        state["core", k].wait_recv()
        for step in (2, 1, 3, 0):
            at = ring_b[k].at(step)
            for way in range(2):
                add_into(dec.at[k, c, at, way], core_in.at[k, at, way])
        ring_b[k].scatter(
            lambda pos, way: dec.at[k, c, pos, way],
            lambda way: b_fwd.at[k, way],
            lambda way: b_own.at[k, way],
            lambda way: b_sum.at[k, way],
        )

    def zm(k):
        ring_b[k].middle()

    def ze(k):
        ring_b[k].finish()
        way = 1 - xl
        gone = dec.at[k, c, z, way]
        gone[...] = (f32(gone[...]) + f32(b_own[k, way]) + f32(b_sum[k, way])).astype(jnp.bfloat16)
        state["xl", k] = kit.send(gone, b_x.at[k], x_near)

    def update(k):
        if k == 0:
            for load in loads["outer"]:
                load.wait()
        state["xl", k].wait_recv()
        rows = pl.ds(k * PART, PART)
        total = f32(dec[k, c, z, xl]) + f32(b_own[k, xl]) + f32(b_sum[k, xl]) + f32(b_x[k])
        step = total / 16
        new_mom = momentum_rate * mo[rows, :] + step
        new_params = pr[rows, :] - outer_rate * (step + momentum_rate * new_mom)
        mo[rows, :] = new_mom
        pr[rows, :] = new_params
        mine = fresh.at[k, c, z, xl]
        mine[...] = new_params.astype(jnp.bfloat16)
        ring_b[k].gather_open(lambda pos, way: fresh.at[k, c, pos, way])
        state["fx", k] = kit.recv_slots(1)
        kit.send(mine, mine, x_near, state["fx", k])
        ring_b[k].gather(xl)
        kit.out(mo.at[rows], mom_o.at[rows])
        kit.out(pr.at[rows], params_o.at[rows])

    def bp(k):
        kit.wait_on(fresh.at[k, c, z, 1 - xl], state["fx", k])
        ring_b[k].gather(1 - xl)

    def bf(k):
        ring_b[k].forward()
        ring_b[k].await_rest()

    def bc(k):
        ring_b[k].await_far()
        state["fc", k] = kit.recv_slots(1)
        mine = fresh.at[k, c]
        kit.send(mine, mine, other, state["fc", k])

    def merge(k):
        kit.wait_on(fresh.at[k, 1 - c], state["fc", k])
        rows = pl.ds(k * PART, PART)
        for target in range(16):
            cols = pl.ds(target * SHARE, SHARE)
            got = fresh[k, target % 2, target // 4, (target // 2) % 2]
            cd[rows, cols] = (mix_rate * f32(w[rows, cols]) + (1.0 - mix_rate) * f32(got)).astype(
                jnp.bfloat16
            )
        kit.out(cd.at[rows], merged_o.at[rows])

    steps = {
        "mm1": mm1, "xadd": xadd, "mid": mid, "end": end, "norm": norm, "agp": agp, "agf": agf, "agx": agx, "mm2": mm2, "mm3": mm3,
        "gg": gain_sum, "dec": decode, "zs": zs, "zm": zm, "ze": ze, "up": update, "bp": bp, "bf": bf, "bc": bc, "mg": merge,
    }
    for name, number in SCHEDULE:
        steps[name](number)
    for wait in kit.open:
        wait()


def place_kernel(*refs):
    count = (len(refs) - 2) // 3
    got, put, held = refs[:count], refs[count : 2 * count], refs[2 * count : 3 * count]
    come, leave = refs[3 * count :]
    pieces = []
    for i in range(count):
        rows = got[i].shape[0]
        step = PLACE_ROWS if rows % PLACE_ROWS == 0 else rows
        pieces += [(i, pl.ds(at, step)) for at in range(0, rows, step)]
    first = [
        pltpu.make_async_copy(got[i].at[rows], held[i].at[rows], come.at[n])
        for n, (i, rows) in enumerate(pieces)
    ]
    second = [
        pltpu.make_async_copy(held[i].at[rows], put[i].at[rows], leave.at[n])
        for n, (i, rows) in enumerate(pieces)
    ]
    for copy in first:
        copy.start()
    for n, copy in enumerate(second):
        first[n].wait()
        copy.start()
    for copy in second:
        copy.wait()


def shards(hidden, inner_down, residual_in, gain, cotangent, codes, scales, outer_params, momentum):
    anywhere = pl.BlockSpec(memory_space=pl.ANY)
    bf, ft = jnp.bfloat16, jnp.float32
    vmem = pltpu.VMEM
    results = pl.pallas_call(
        sync_kernel,
        out_shape=(
            jax.ShapeDtypeStruct(residual_in.shape, bf),
            jax.ShapeDtypeStruct(hidden.shape, bf),
            jax.ShapeDtypeStruct((1, D), ft),
            jax.ShapeDtypeStruct(outer_params.shape, ft),
            jax.ShapeDtypeStruct(momentum.shape, ft),
            jax.ShapeDtypeStruct(codes.shape[1:], bf),
        ),
        in_specs=[pl.BlockSpec(memory_space=pltpu.HBM)] * 9,
        out_specs=(anywhere,) * 6,
        scratch_shapes=[
            vmem((UNITS, D), bf),
            vmem((512, UNITS), bf),
            vmem((8 * ROWS, UNITS), bf),
            vmem((CHUNKS, 4, 2, ROWS, D), bf),
            vmem((CHUNKS, 2, ROWS, D), bf),
            vmem((CHUNKS, 2, ROWS, D), bf),
            vmem((CHUNKS, 2, ROWS, D), bf),
            vmem((CHUNKS, ROWS, D), bf),
            vmem((4, ROWS, D), bf),
            vmem((CHUNKS, 4, 2, ROWS, D), bf),
            vmem((64, D), bf),
            vmem((64, D), bf),
            vmem((1, D), ft),
            vmem((ROWS, D), ft),
            vmem((64, D), bf),
            vmem((512, UNITS), bf),
            vmem((8, D), ft),
            vmem((4, 1, D), ft),
            vmem((3, 1, D), ft),
            vmem((FRAG_ROWS, D), bf),
            vmem((D // BLOCK, FRAG_ROWS), ft),
            vmem((PARTS, 2, 4, 2, PART, SHARE), bf),
            vmem((PARTS, 4, 2, PART, SHARE), bf),
            vmem((PARTS, 2, PART, SHARE), bf),
            vmem((PARTS, 2, PART, SHARE), bf),
            vmem((PARTS, 2, PART, SHARE), bf),
            vmem((PARTS, PART, SHARE), bf),
            vmem((PARTS, 2, 4, 2, PART, SHARE), bf),
            vmem((FRAG_ROWS, SHARE), ft),
            vmem((FRAG_ROWS, SHARE), ft),
            pltpu.SemaphoreType.DMA((N_SEND,)),
            pltpu.SemaphoreType.DMA((N_RECV,)),
            pltpu.SemaphoreType.DMA((N_LOCAL,)),
        ],
        compiler_params=pltpu.CompilerParams(
            collective_id=0, has_side_effects=True, vmem_limit_bytes=60 * 2**20
        ),
        cost_estimate=pl.CostEstimate(
            flops=4 * 512 * UNITS * D, bytes_accessed=28 * 2**20, transcendentals=0
        ),
        name="sync_step",
    )(
        hidden,
        inner_down[0],
        residual_in,
        gain.reshape(1, D),
        cotangent,
        codes[0],
        scales[0].T,
        outer_params,
        momentum,
    )
    normed, grad_hidden, grad_gain, new_params, new_momentum, merged = pl.pallas_call(
        place_kernel,
        out_shape=tuple(jax.ShapeDtypeStruct(v.shape, v.dtype) for v in results),
        in_specs=[anywhere] * 6,
        out_specs=(anywhere,) * 6,
        scratch_shapes=[pltpu.VMEM(v.shape, v.dtype) for v in results]
        + [pltpu.SemaphoreType.DMA((24,)), pltpu.SemaphoreType.DMA((24,))],
        compiler_params=pltpu.CompilerParams(vmem_limit_bytes=60 * 2**20),
        name="place_results",
    )(*results)
    return (normed, grad_hidden, grad_gain, new_params, new_momentum, merged[None])


def solution(mesh):
    placed = (
        P("replica", "mp"),
        P("replica", "mp", None),
        P(("replica", "mp"), None),
        P(),
        P(("replica", "mp"), None),
        P("replica", "mp", None),
        P("replica", "mp", None),
        P("mp", "replica"),
        P("mp", "replica"),
    )
    return jax.shard_map(
        shards,
        mesh=mesh,
        in_specs=placed,
        out_specs=(
            P(("replica", "mp"), None),
            P("replica", "mp"),
            P("replica", None),
            P("mp", "replica"),
            P("mp", "replica"),
            P("replica", "mp", None),
        ),
        check_vma=False,
    )
```

time: 473 us -> 90 us (0.19)
  waiting for transfers between devices: 406 us -> 0 us
  Pallas kernels: 0 us -> 89.1 us
  other arithmetic: 30.8 us -> 0 us
  matrix products: 17.9 us -> 0 us
  between operations: 13.9 us -> 0.8 us
    psum x2 -> x0, waiting for transfers between devices: 239 us -> none  [the longest x1 127 us: shards(): lax.psum(decode(codes[0], scales[0]).astype(jnp.bfloat16), 'replica')]
    all_gather x3 -> x0, waiting for transfers between devices: 166 us -> none  [the longest x1 72 us: shards(): lax.all_gather(residual_in, 'mp', axis=0, tiled=True)]
    pallas_call x0 -> x2, Pallas kernels: none -> 89.1 us  [the longest x1 83.1 us: shards(): pl.pallas_call(sync_kernel, out_shape=(jax.ShapeDtypeStruct(residual_in.s...]
    dot_general x2 -> x0, matrix products: 17.9 us -> none  [the longest x1 9.27 us: shards(): jnp.dot(hidden, weights, preferred_element_type=jnp.float32) * scale_ff]
    reduce_sum x2 -> x0, other arithmetic: 13.4 us -> none  [the longest x1 8.51 us: shards(): grad_gain = jnp.sum(cot_all.astype(jnp.float32) * unit_rows, 0)]
    convert_element_type x3 -> x0, other arithmetic: 10.1 us -> none  [the longest x1 7.12 us: shards(): decode(codes[0], scales[0]).astype(jnp.bfloat16)]
    broadcast_in_dim x1 -> x0, other arithmetic: 7.22 us -> none  [shards(): merged[None]]
  transfers between devices with their start and end apart: 5 -> 0, of which waited for: 5 -> 0; matrix products, arithmetic and copies ran while one was open for 7% -> 0% of each run, Pallas kernels for 0% -> 0%
where the time goes in v1:
time: 90 us; the launch traced here: 89.9 us
  Pallas kernels  89.1 us (99%)
    pallas_call x1, Pallas kernels, shards(): pl.pallas_call(sync_kernel, out_shape=(jax.ShapeDtypeStruct(residual_in.s...  83.1 us
    pallas_call x1, Pallas kernels, shards(): pl.pallas_call(place_kernel, out_shape=tuple((jax.ShapeDtypeStruct(v.shap...  5.93 us

profile of v1, /device:TPU:1, one launch (start us, length us, event | category | flops | bytes accessed | tf_op | source)
XLA Modules:
  0.0 89.9 jit_solution(14780737924756311769)
XLA Ops:
  0.6 83.1 %sync_step.1 = (bf16[64,4096]{1,0:T(8,128)(2,1)}, bf16[512,896]{1,0:T(8,128)(2,1)}, f32[1,4096]{1,0:T(1,128)}, f32[512,256]{1,0:T(8,128)}, f32[512,256]{1,0:T(8,128)}, /*index=5*/bf16[512,4096]{1,0:T(8,128)(2,1)}) custom-call(bf16[512,896]{1,0:T(8,128)(2,1)} %hidden.1, bf16[896,4096]{1,0:T(8,128)(2,1)} %bitcast.7, bf16[64,4096]{1,0:T(8,128)(2,1)} %resid.1, ...), custom_call_target="tpu_custom_call" | custom-call | flops 7516192768 | bytes 29360128 | tf_op jit(solution)/shard_map/sync_step/pallas_call | solution.py:509
  83.8 5.9 %place_results.1 = (bf16[64,4096]{1,0:T(8,128)(2,1)}, bf16[512,896]{1,0:T(8,128)(2,1)}, f32[1,4096]{1,0:T(1,128)}, f32[512,256]{1,0:T(8,128)}, f32[512,256]{1,0:T(8,128)}, /*index=5*/bf16[512,4096]{1,0:T(8,128)(2,1)}) custom-call(bf16[64,4096]{1,0:T(8,128)(2,1)} %get-tuple-element.18.refs_0_, bf16[512,896]{1,0:T(8,128)(2,1)} %get-tuple-element.19.refs_1_, ...), custom_call_target="tpu_custom_call" | custom-call | tf_op jit(solution)/shard_map/place_results/pallas_call | solution.py:574

commit v2 on v1

--- a/solution.py
+++ b/solution.py
@@ -19,6 +19,7 @@
 UNITS = 896
 ROWS = 16
 CHUNKS = 4
+COL_PARTS = (1, 1, 1, 2)
 PARTS = 2
 FRAG_ROWS = 512
 PART = FRAG_ROWS // PARTS
@@ -26,18 +27,17 @@
 HALF = D // 2
 X_FIRST = (False, True, False, False)
 CUT = 512
-PLACE_ROWS = 128
 N_SEND, N_RECV, N_LOCAL = 160, 160, 40
 
 SCHEDULE = (
-    ("mm1", 0), ("dec", 0), ("mm1", 1), ("mm1", 2), ("zs", 0), ("mid", 0), ("mm1", 3), ("dec", 1),
-    ("zm", 0), ("zs", 1), ("mid", 2), ("ze", 0), ("xadd", 1), ("end", 0), ("zm", 1), ("mid", 3),
-    ("up", 0), ("ze", 1), ("norm", 0), ("end", 2), ("mid", 1), ("bp", 0), ("up", 1), ("end", 3),
-    ("bf", 0), ("agp", 0), ("end", 1), ("norm", 1), ("norm", 2), ("agf", 0), ("bc", 0), ("bp", 1),
-    ("mg", 0), ("norm", 3), ("gg", 0), ("agf", 1), ("bf", 1), ("agx", 0), ("agp", 2), ("gg", 1),
-    ("mm2", 0), ("bc", 1), ("agp", 3), ("agx", 1), ("mm3", 0), ("gg", 2), ("mg", 1), ("agf", 2),
-    ("agf", 3), ("mm2", 1), ("agx", 2), ("gg", 3), ("mm2", 2), ("mm3", 1), ("agx", 3), ("mm2", 3),
-    ("mm3", 3), ("mm3", 2),
+    ("mm1", 0), ("mm1", 1), ("dec", 0), ("dec", 1), ("zs", 0), ("mid", 0), ("zs", 1), ("mm1", 2),
+    ("mm1", 3), ("zm", 0), ("end", 0), ("mid", 2), ("xadd", 1), ("zm", 1), ("mid", 3), ("norm", 0),
+    ("mid", 13), ("ze", 0), ("agp", 0), ("ze", 1), ("end", 2), ("mid", 1), ("up", 0), ("end", 3),
+    ("up", 1), ("norm", 2), ("end", 13), ("bp", 0), ("agf", 0), ("end", 1), ("norm", 1), ("bp", 1),
+    ("bf", 0), ("agp", 2), ("agx", 0), ("norm", 3), ("gg", 0), ("bf", 1), ("agf", 1), ("mm2", 0),
+    ("bc", 0), ("gg", 1), ("agf", 2), ("agp", 3), ("mm3", 0), ("agp", 13), ("bc", 1), ("mg", 0),
+    ("gg", 2), ("mg", 1), ("agx", 1), ("agx", 2), ("mm2", 2), ("agf", 3), ("mm3", 2), ("gg", 3),
+    ("agf", 13), ("mm2", 1), ("agx", 3), ("mm3", 1), ("agx", 13), ("mm2", 3), ("mm3", 3),
 )
 
 
@@ -144,9 +144,6 @@
         copy.start()
         return copy
 
-    def out(self, src, dst):
-        self.open.append(self.local(src, dst).wait)
-
 
 def f32(value):
     return value.astype(jnp.float32)
@@ -158,9 +155,9 @@
 
 def sync_kernel(
     hidden, weights, resid, gain, cot, codes, scales, params, mom,
-    normed_o, hgrad_o, ggain_o, params_o, mom_o, merged_o,
-    w, hid, lhs, prod, a_fwd, a_own, a_sum, a_x, a_x4, gm, res, ct, gn, mixed, nrm, hg, gg, gs, gr,
-    cd, sc, dec, core_in, b_fwd, b_own, b_sum, b_x, fresh, pr, mo,
+    nrm, hg, gsum, pr, mo, cd,
+    w, hid, lhs, prod, a_fwd, a_own, a_sum, a_x, a_x4, gm, res, ct, gn, mixed, gg, gs, gr,
+    sc, dec, core_in, b_fwd, b_own, b_sum, b_x, fresh,
     ssem, rsem, lsem,
 ):
     kit = Kit(ssem, rsem, lsem)
@@ -197,7 +194,7 @@
         pl.semaphore_signal(barrier, inc=1, device_id=peer, device_id_type=MESH)
 
     scale_ff = FF ** (-0.5)
-    ring_a = [Ring(kit, y, y_next, y_prev) for _ in range(CHUNKS)]
+    ring_a = {}
     ring_b = [Ring(kit, z, z_next, z_prev) for _ in range(PARTS)]
     state = {}
     load_hid.wait()
@@ -205,20 +202,27 @@
     def half(k):
         return pl.ds(k * HALF, HALF)
 
+    def part_of(i, p):
+        return pl.ds(p * (D // COL_PARTS[i]), D // COL_PARTS[i])
+
     def ring_start(i):
         if X_FIRST[i]:
+            ring_a[i] = Ring(kit, y, y_next, y_prev)
             ring_a[i].scatter(
                 lambda pos, k: prod.at[i, pos, xh, :, half(k)],
                 lambda k: a_fwd.at[i, 0, :, half(k)],
                 lambda k: a_own.at[i, 0, :, half(k)],
                 lambda k: a_sum.at[i, 0, :, half(k)],
             )
-        else:
-            ring_a[i].scatter(
-                lambda pos, k: prod.at[i, pos, k],
-                lambda k: a_fwd.at[i, k],
-                lambda k: a_own.at[i, k],
-                lambda k: a_sum.at[i, k],
+            return
+        for p in range(COL_PARTS[i]):
+            cols = part_of(i, p)
+            ring_a[i + 10 * p] = Ring(kit, y, y_next, y_prev)
+            ring_a[i + 10 * p].scatter(
+                lambda pos, k, cols=cols: prod.at[i, pos, k, :, cols],
+                lambda k, cols=cols: a_fwd.at[i, k, :, cols],
+                lambda k, cols=cols: a_own.at[i, k, :, cols],
+                lambda k, cols=cols: a_sum.at[i, k, :, cols],
             )
 
     def mm1(i):
@@ -254,21 +258,24 @@
     def mid(i):
         ring_a[i].middle()
 
-    def end(i):
-        ring_a[i].finish()
+    def end(number):
+        p, i = divmod(number, 10)
+        ring_a[number].finish()
         if X_FIRST[i]:
             return
-        k = 1 - xh
-        gone = prod.at[i, y, k]
-        gone[...] = (f32(gone[...]) + f32(a_own[i, k]) + f32(a_sum[i, k])).astype(jnp.bfloat16)
-        state["x", i] = kit.send(gone, a_x.at[i], x_far)
+        k, cols = 1 - xh, part_of(i, p)
+        gone = prod.at[i, y, k, :, cols]
+        total = f32(gone[...]) + f32(a_own[i, k, :, cols]) + f32(a_sum[i, k, :, cols])
+        gone[...] = total.astype(jnp.bfloat16)
+        state["x", number] = kit.send(gone, a_x.at[i, :, cols], x_far)
 
     def norm(i):
         if i == 0:
             for load in loads["norm"]:
                 load.wait()
         if not X_FIRST[i]:
-            state["x", i].wait_recv()
+            for p in range(COL_PARTS[i]):
+                state["x", i + 10 * p].wait_recv()
         rows = pl.ds(i * ROWS, ROWS)
         step = D // 4
         square = jnp.zeros((ROWS, 1), jnp.float32)
@@ -312,34 +319,39 @@
             mine = gm.at[i, y, xh]
             kit.send(mine, mine, x_far, state["gx", i] + y)
         else:
-            ring_a[i].gather_open(lambda pos, k: gm.at[i, pos, k])
-            mine = gm.at[i, y, xh]
-            state["gx", i] = kit.recv_slots(1)
-            kit.send(mine, mine, x_far, state["gx", i])
-            ring_a[i].gather(xh)
-        if i == CHUNKS - 1:
-            kit.out(nrm, normed_o)
-
-    def agp(i):
+            for p in range(COL_PARTS[i]):
+                number, cols = i + 10 * p, part_of(i, p)
+                ring_a[number].gather_open(lambda pos, k, cols=cols: gm.at[i, pos, k, :, cols])
+                mine = gm.at[i, y, xh, :, cols]
+                state["gx", number] = kit.recv_slots(1)
+                kit.send(mine, mine, x_far, state["gx", number])
+                ring_a[number].gather(xh)
+
+    def agp(number):
+        p, i = divmod(number, 10)
         if not X_FIRST[i]:
-            kit.wait_on(gm.at[i, y, 1 - xh], state["gx", i])
-            ring_a[i].gather(1 - xh)
-
-    def agf(i):
-        ring = ring_a[i]
+            kit.wait_on(gm.at[i, y, 1 - xh, :, part_of(i, p)], state["gx", number])
+            ring_a[number].gather(1 - xh)
+
+    def agf(number):
+        p, i = divmod(number, 10)
+        ring = ring_a[number]
         ring.forward()
-        ring.await_rest()
-        if X_FIRST[i]:
+        if X_FIRST[i]:
+            ring.await_rest()
             for step in (1, 3):
                 there = gm.at[i, ring.at(step), xh]
                 kit.send(there, there, x_far, state["gx", i] + ring.at(step))
 
-    def agx(i):
-        ring = ring_a[i]
+    def agx(number):
+        p, i = divmod(number, 10)
+        ring = ring_a[number]
         ring.await_far()
         if X_FIRST[i]:
             there = gm.at[i, ring.at(2), xh]
             kit.send(there, there, x_far, state["gx", i] + ring.at(2))
+        else:
+            ring.await_rest()
 
     def back(i, first, count):
         units = pl.ds(first, count)
@@ -354,9 +366,6 @@
             for xx in range(2):
                 at = (yy * 2 + xx) * ROWS
                 hg[pl.ds((xx * 4 + yy) * 64 + i * ROWS, ROWS), units] = out[at : at + ROWS]
-        state["hg"] = state.get("hg", 0) + 1
-        if state["hg"] == 2 * CHUNKS:
-            kit.out(hg, hgrad_o)
 
     def mm2(i):
         if X_FIRST[i]:
@@ -381,7 +390,7 @@
         if step < 3:
             state["gg", step] = kit.send(gs.at[step], gr.at[step], partner)
         else:
-            kit.out(gs.at[3], ggain_o)
+            gsum[...] = gs[3]
 
     def decode(k):
         if k == 0:
@@ -438,8 +447,6 @@
         state["fx", k] = kit.recv_slots(1)
         kit.send(mine, mine, x_near, state["fx", k])
         ring_b[k].gather(xl)
-        kit.out(mo.at[rows], mom_o.at[rows])
-        kit.out(pr.at[rows], params_o.at[rows])
 
     def bp(k):
         kit.wait_on(fresh.at[k, c, z, 1 - xl], state["fx", k])
@@ -464,7 +471,6 @@
             cd[rows, cols] = (mix_rate * f32(w[rows, cols]) + (1.0 - mix_rate) * f32(got)).astype(
                 jnp.bfloat16
             )
-        kit.out(cd.at[rows], merged_o.at[rows])
 
     steps = {
         "mm1": mm1, "xadd": xadd, "mid": mid, "end": end, "norm": norm, "agp": agp, "agf": agf, "agx": agx, "mm2": mm2, "mm3": mm3,
@@ -477,28 +483,12 @@
 
 
 def place_kernel(*refs):
-    count = (len(refs) - 2) // 3
-    got, put, held = refs[:count], refs[count : 2 * count], refs[2 * count : 3 * count]
-    come, leave = refs[3 * count :]
-    pieces = []
-    for i in range(count):
-        rows = got[i].shape[0]
-        step = PLACE_ROWS if rows % PLACE_ROWS == 0 else rows
-        pieces += [(i, pl.ds(at, step)) for at in range(0, rows, step)]
-    first = [
-        pltpu.make_async_copy(got[i].at[rows], held[i].at[rows], come.at[n])
-        for n, (i, rows) in enumerate(pieces)
-    ]
-    second = [
-        pltpu.make_async_copy(held[i].at[rows], put[i].at[rows], leave.at[n])
-        for n, (i, rows) in enumerate(pieces)
-    ]
-    for copy in first:
+    sems = refs[-1]
+    count = (len(refs) - 1) // 2
+    copies = [pltpu.make_async_copy(refs[i], refs[count + i], sems.at[i]) for i in range(count)]
+    for copy in copies:
         copy.start()
-    for n, copy in enumerate(second):
-        first[n].wait()
-        copy.start()
-    for copy in second:
+    for copy in copies:
         copy.wait()
 
 
@@ -509,15 +499,15 @@
     results = pl.pallas_call(
         sync_kernel,
         out_shape=(
-            jax.ShapeDtypeStruct(residual_in.shape, bf),
-            jax.ShapeDtypeStruct(hidden.shape, bf),
-            jax.ShapeDtypeStruct((1, D), ft),
-            jax.ShapeDtypeStruct(outer_params.shape, ft),
-            jax.ShapeDtypeStruct(momentum.shape, ft),
-            jax.ShapeDtypeStruct(codes.shape[1:], bf),
+            vmem(residual_in.shape, bf),
+            vmem(hidden.shape, bf),
+            vmem((1, D), ft),
+            vmem(outer_params.shape, ft),
+            vmem(momentum.shape, ft),
+            vmem(codes.shape[1:], bf),
         ),
         in_specs=[pl.BlockSpec(memory_space=pltpu.HBM)] * 9,
-        out_specs=(anywhere,) * 6,
+        out_specs=(pl.BlockSpec(memory_space=pltpu.VMEM),) * 6,
         scratch_shapes=[
             vmem((UNITS, D), bf),
             vmem((512, UNITS), bf),
@@ -533,12 +523,9 @@
             vmem((64, D), bf),
             vmem((1, D), ft),
             vmem((ROWS, D), ft),
-            vmem((64, D), bf),
-            vmem((512, UNITS), bf),
             vmem((8, D), ft),
             vmem((4, 1, D), ft),
             vmem((3, 1, D), ft),
-            vmem((FRAG_ROWS, D), bf),
             vmem((D // BLOCK, FRAG_ROWS), ft),
             vmem((PARTS, 2, 4, 2, PART, SHARE), bf),
             vmem((PARTS, 4, 2, PART, SHARE), bf),
@@ -547,14 +534,12 @@
             vmem((PARTS, 2, PART, SHARE), bf),
             vmem((PARTS, PART, SHARE), bf),
             vmem((PARTS, 2, 4, 2, PART, SHARE), bf),
-            vmem((FRAG_ROWS, SHARE), ft),
-            vmem((FRAG_ROWS, SHARE), ft),
             pltpu.SemaphoreType.DMA((N_SEND,)),
             pltpu.SemaphoreType.DMA((N_RECV,)),
             pltpu.SemaphoreType.DMA((N_LOCAL,)),
         ],
         compiler_params=pltpu.CompilerParams(
-            collective_id=0, has_side_effects=True, vmem_limit_bytes=60 * 2**20
+            collective_id=0, has_side_effects=True, vmem_limit_bytes=56 * 2**20
         ),
         cost_estimate=pl.CostEstimate(
             flops=4 * 512 * UNITS * D, bytes_accessed=28 * 2**20, transcendentals=0
@@ -574,11 +559,10 @@
     normed, grad_hidden, grad_gain, new_params, new_momentum, merged = pl.pallas_call(
         place_kernel,
         out_shape=tuple(jax.ShapeDtypeStruct(v.shape, v.dtype) for v in results),
-        in_specs=[anywhere] * 6,
+        in_specs=[pl.BlockSpec(memory_space=pltpu.VMEM)] * 6,
         out_specs=(anywhere,) * 6,
-        scratch_shapes=[pltpu.VMEM(v.shape, v.dtype) for v in results]
-        + [pltpu.SemaphoreType.DMA((24,)), pltpu.SemaphoreType.DMA((24,))],
-        compiler_params=pltpu.CompilerParams(vmem_limit_bytes=60 * 2**20),
+        scratch_shapes=[pltpu.SemaphoreType.DMA((6,))],
+        compiler_params=pltpu.CompilerParams(vmem_limit_bytes=2**20),
         name="place_results",
     )(*results)
     return (normed, grad_hidden, grad_gain, new_params, new_momentum, merged[None])

time: 90 us -> 84.4 us (0.938)
  Pallas kernels: 89.1 us -> 83.5 us
    pallas_call x1, Pallas kernels: 5.93 us -> 2.89 us  [shards(): pl.pallas_call(place_kernel, out_shape=tuple((jax.ShapeDtypeStruct(v.shap...]
    pallas_call x1, Pallas kernels: 83.1 us -> 80.6 us  [shards(): pl.pallas_call(sync_kernel, out_shape=(vmem(residual_in.shape, bf), vmem(...]
where the time goes in v2:
time: 84.4 us; the launch traced here: 84.3 us
  Pallas kernels  83.5 us (99%)
    pallas_call x1, Pallas kernels, shards(): pl.pallas_call(sync_kernel, out_shape=(vmem(residual_in.shape, bf), vmem(...  80.6 us
    pallas_call x1, Pallas kernels, shards(): pl.pallas_call(place_kernel, out_shape=tuple((jax.ShapeDtypeStruct(v.shap...  2.89 us

profile of v2, /device:TPU:1, one launch (start us, length us, event | category | flops | bytes accessed | tf_op | source)
XLA Modules:
  0.0 84.3 jit_solution(4913101517713258320)
XLA Ops:
  0.6 80.6 %sync_step.1 = (bf16[64,4096]{1,0:T(8,128)(2,1)S(1)}, bf16[512,896]{1,0:T(8,128)(2,1)S(1)}, f32[1,4096]{1,0:T(1,128)S(1)}, f32[512,256]{1,0:T(8,128)S(1)}, f32[5...) custom-call(bf16[512,896]{1,0:T(8,128)(2,1)} %hidden.1, bf16[896,4096]{1,0:T(8,128)(2,1)} %bitcast.7, ...), custom_call_target="tpu_custom_call" | custom-call | flops 7516192768 | bytes 29360128 | tf_op jit(solution)/shard_map/sync_step/pallas_call | solution.py:499
  81.2 2.9 %place_results.1 = (bf16[64,4096]{1,0:T(8,128)(2,1)}, bf16[512,896]{1,0:T(8,128)(2,1)}, f32[1,4096]{1,0:T(1,128)}, f32[512,256]{1,0:T(8,128)}, f32[512,256]{1,0:T(8,128)}, /*index=5*/bf16[512,4096]{1,0:T(8,128)(2,1)}) custom-call(bf16[64,4096]{1,0:T(8,128)(2,1)S(1)} %get-tuple-element.18.refs_0_, bf16[512,896]{1,0:T(8,128)(2,1)S(1)} %get-tuple-element.19.refs_1_, ...), custom_call_target="tpu_custom_call" | custom-call | tf_op jit(solution)/shard_map/place_results/pallas_call | solution.py:559

commit v3 on v2

--- a/solution.py
+++ b/solution.py
@@ -19,7 +19,7 @@
 UNITS = 896
 ROWS = 16
 CHUNKS = 4
-COL_PARTS = (1, 1, 1, 2)
+COL_PARTS = (2, 1, 2, 2)
 PARTS = 2
 FRAG_ROWS = 512
 PART = FRAG_ROWS // PARTS
@@ -30,14 +30,16 @@
 N_SEND, N_RECV, N_LOCAL = 160, 160, 40
 
 SCHEDULE = (
-    ("mm1", 0), ("mm1", 1), ("dec", 0), ("dec", 1), ("zs", 0), ("mid", 0), ("zs", 1), ("mm1", 2),
-    ("mm1", 3), ("zm", 0), ("end", 0), ("mid", 2), ("xadd", 1), ("zm", 1), ("mid", 3), ("norm", 0),
-    ("mid", 13), ("ze", 0), ("agp", 0), ("ze", 1), ("end", 2), ("mid", 1), ("up", 0), ("end", 3),
-    ("up", 1), ("norm", 2), ("end", 13), ("bp", 0), ("agf", 0), ("end", 1), ("norm", 1), ("bp", 1),
-    ("bf", 0), ("agp", 2), ("agx", 0), ("norm", 3), ("gg", 0), ("bf", 1), ("agf", 1), ("mm2", 0),
-    ("bc", 0), ("gg", 1), ("agf", 2), ("agp", 3), ("mm3", 0), ("agp", 13), ("bc", 1), ("mg", 0),
-    ("gg", 2), ("mg", 1), ("agx", 1), ("agx", 2), ("mm2", 2), ("agf", 3), ("mm3", 2), ("gg", 3),
-    ("agf", 13), ("mm2", 1), ("agx", 3), ("mm3", 1), ("agx", 13), ("mm2", 3), ("mm3", 3),
+    ("mm1", 0), ("mm1", 1), ("dec", 1), ("mid", 0), ("zs", 1), ("mid", 10), ("dec", 0), ("mm1", 2),
+    ("end", 0), ("zs", 0), ("end", 10), ("zm", 1), ("mid", 2), ("mm1", 3), ("mid", 12), ("xadd", 1),
+    ("zm", 0), ("end", 2), ("norm", 0), ("mid", 3), ("mid", 13), ("ze", 1), ("agp", 0), ("end", 12),
+    ("ze", 0), ("agp", 10), ("mid", 1), ("up", 1), ("norm", 2), ("end", 3), ("up", 0), ("end", 13),
+    ("agf", 0), ("bp", 1), ("agf", 10), ("agp", 2), ("end", 1), ("norm", 1), ("agp", 12), ("agx", 0),
+    ("bp", 0), ("agx", 10), ("norm", 3), ("gg", 0), ("mm2", 0), ("bf", 1), ("mm3", 0), ("agf", 2),
+    ("agf", 1), ("gg", 1), ("bf", 0), ("agf", 12), ("agp", 3), ("agp", 13), ("bc", 1), ("agx", 2),
+    ("mm2", 2), ("gg", 2), ("agx", 1), ("mg", 1), ("bc", 0), ("agx", 12), ("mm3", 2), ("agf", 3),
+    ("gg", 3), ("mg", 0), ("agf", 13), ("mm2", 1), ("agx", 3), ("mm2", 3), ("agx", 13), ("mm3", 3),
+    ("mm3", 1),
 )
 
 
@@ -156,7 +158,7 @@
 def sync_kernel(
     hidden, weights, resid, gain, cot, codes, scales, params, mom,
     nrm, hg, gsum, pr, mo, cd,
-    w, hid, lhs, prod, a_fwd, a_own, a_sum, a_x, a_x4, gm, res, ct, gn, mixed, gg, gs, gr,
+    w, hid, lhs, prod, a_fwd, a_own, a_sum, a_x, a_x4, gm, res, ct, gn, mixed, acc, gg, gs, gr,
     sc, dec, core_in, b_fwd, b_own, b_sum, b_x, fresh,
     ssem, rsem, lsem,
 ):
@@ -205,7 +207,7 @@
     def part_of(i, p):
         return pl.ds(p * (D // COL_PARTS[i]), D // COL_PARTS[i])
 
-    def ring_start(i):
+    def ring_start(i, p=0):
         if X_FIRST[i]:
             ring_a[i] = Ring(kit, y, y_next, y_prev)
             ring_a[i].scatter(
@@ -215,15 +217,14 @@
                 lambda k: a_sum.at[i, 0, :, half(k)],
             )
             return
-        for p in range(COL_PARTS[i]):
-            cols = part_of(i, p)
-            ring_a[i + 10 * p] = Ring(kit, y, y_next, y_prev)
-            ring_a[i + 10 * p].scatter(
-                lambda pos, k, cols=cols: prod.at[i, pos, k, :, cols],
-                lambda k, cols=cols: a_fwd.at[i, k, :, cols],
-                lambda k, cols=cols: a_own.at[i, k, :, cols],
-                lambda k, cols=cols: a_sum.at[i, k, :, cols],
-            )
+        cols = part_of(i, p)
+        ring_a[i + 10 * p] = Ring(kit, y, y_next, y_prev)
+        ring_a[i + 10 * p].scatter(
+            lambda pos, k: prod.at[i, pos, k, :, cols],
+            lambda k: a_fwd.at[i, k, :, cols],
+            lambda k: a_own.at[i, k, :, cols],
+            lambda k: a_sum.at[i, k, :, cols],
+        )
 
     def mm1(i):
         for yy in range(4):
@@ -238,14 +239,14 @@
             out = jnp.dot(lhs[...], w[:, cols], preferred_element_type=jnp.float32)
             out = (out * scale_ff).astype(jnp.bfloat16)
             prod[i, :, :, :, cols] = out.reshape(4, 2, ROWS, width)
+            if i == 0 and q == 4 // COL_PARTS[i] - 1:
+                pl.semaphore_wait(barrier, len(peers))
+            if not X_FIRST[i] and (q + 1) * COL_PARTS[i] % 4 == 0:
+                ring_start(i, (q + 1) * COL_PARTS[i] // 4 - 1)
         if i == 0:
             load_rest()
-            pl.semaphore_wait(barrier, len(peers))
-
         if X_FIRST[i]:
             state["x4", i] = kit.send(prod.at[i, :, 1 - xh], a_x4, x_far)
-        else:
-            ring_start(i)
 
     def xadd(i):
         if not X_FIRST[i]:
@@ -270,9 +271,8 @@
         state["x", number] = kit.send(gone, a_x.at[i, :, cols], x_far)
 
     def norm(i):
-        if i == 0:
-            for load in loads["norm"]:
-                load.wait()
+        for load in loads.pop("norm", ()):
+            load.wait()
         if not X_FIRST[i]:
             for p in range(COL_PARTS[i]):
                 state["x", i + 10 * p].wait_recv()
@@ -353,14 +353,15 @@
         else:
             ring.await_rest()
 
-    def back(i, first, count):
-        units = pl.ds(first, count)
-        out = lax.dot_general(
-            w[units, :],
-            gm[i].reshape(8 * ROWS, D),
+    def back(i, units, cols):
+        return lax.dot_general(
+            w[units, cols],
+            gm[i, :, :, :, cols].reshape(8 * ROWS, cols.size),
             (((1,), (1,)), ((), ())),
             preferred_element_type=jnp.float32,
         )
+
+    def back_out(i, units, out):
         out = (out * scale_ff).T.astype(jnp.bfloat16)
         for yy in range(4):
             for xx in range(2):
@@ -371,10 +372,19 @@
         if X_FIRST[i]:
             for pos in range(4):
                 kit.wait_on(gm.at[i, pos, 1 - xh], state["gx", i] + pos)
-        back(i, 0, CUT)
+        if COL_PARTS[i] == 2:
+            acc[i] = back(i, pl.ds(0, UNITS), half(0))
+        else:
+            units = pl.ds(0, CUT)
+            back_out(i, units, back(i, units, pl.ds(0, D)))
 
     def mm3(i):
-        back(i, CUT, UNITS - CUT)
+        if COL_PARTS[i] == 2:
+            units = pl.ds(0, UNITS)
+            back_out(i, units, acc[i] + back(i, units, half(1)))
+        else:
+            units = pl.ds(CUT, UNITS - CUT)
+            back_out(i, units, back(i, units, pl.ds(0, D)))
 
     def gain_sum(step):
         partner = (x_far, None, None)[step] if step < 1 else None
@@ -393,8 +403,8 @@
             gsum[...] = gs[3]
 
     def decode(k):
-        if k == 0:
-            loads["sc"].wait()
+        if "sc" in loads:
+            loads.pop("sc").wait()
         loads["cd", k].wait()
         rows = pl.ds(k * PART, PART)
         factors = sc[:, rows].T
@@ -430,9 +440,8 @@
         state["xl", k] = kit.send(gone, b_x.at[k], x_near)
 
     def update(k):
-        if k == 0:
-            for load in loads["outer"]:
-                load.wait()
+        for load in loads.pop("outer", ()):
+            load.wait()
         state["xl", k].wait_recv()
         rows = pl.ds(k * PART, PART)
         total = f32(dec[k, c, z, xl]) + f32(b_own[k, xl]) + f32(b_sum[k, xl]) + f32(b_x[k])
@@ -523,6 +532,7 @@
             vmem((64, D), bf),
             vmem((1, D), ft),
             vmem((ROWS, D), ft),
+            vmem((CHUNKS, UNITS, 8 * ROWS), ft),
             vmem((8, D), ft),
             vmem((4, 1, D), ft),
             vmem((3, 1, D), ft),

time: 84.4 us -> 83.6 us (level)
  no operation moved by 1% of the time
where the time goes in v3:
time: 83.6 us; the launch traced here: 83.5 us
  Pallas kernels  82.7 us (99%)
    pallas_call x1, Pallas kernels, shards(): pl.pallas_call(sync_kernel, out_shape=(vmem(residual_in.shape, bf), vmem(...  79.8 us
    pallas_call x1, Pallas kernels, shards(): pl.pallas_call(place_kernel, out_shape=tuple((jax.ShapeDtypeStruct(v.shap...  2.89 us

profile of v3, /device:TPU:1, one launch (start us, length us, event | category | flops | bytes accessed | tf_op | source)
XLA Modules:
  0.0 83.5 jit_solution(16101991593339752999)
XLA Ops:
  0.6 79.8 %sync_step.1 = (bf16[64,4096]{1,0:T(8,128)(2,1)S(1)}, bf16[512,896]{1,0:T(8,128)(2,1)S(1)}, f32[1,4096]{1,0:T(1,128)S(1)}, f32[512,256]{1,0:T(8,128)S(1)}, f32[5...) custom-call(bf16[512,896]{1,0:T(8,128)(2,1)} %hidden.1, bf16[896,4096]{1,0:T(8,128)(2,1)} %bitcast.7, ...), custom_call_target="tpu_custom_call" | custom-call | flops 7516192768 | bytes 29360128 | tf_op jit(solution)/shard_map/sync_step/pallas_call | solution.py:508
  80.4 2.9 %place_results.1 = (bf16[64,4096]{1,0:T(8,128)(2,1)}, bf16[512,896]{1,0:T(8,128)(2,1)}, f32[1,4096]{1,0:T(1,128)}, f32[512,256]{1,0:T(8,128)}, f32[512,256]{1,0:T(8,128)}, /*index=5*/bf16[512,4096]{1,0:T(8,128)(2,1)}) custom-call(bf16[64,4096]{1,0:T(8,128)(2,1)S(1)} %get-tuple-element.18.refs_0_, bf16[512,896]{1,0:T(8,128)(2,1)S(1)} %get-tuple-element.19.refs_1_, ...), custom_call_target="tpu_custom_call" | custom-call | tf_op jit(solution)/shard_map/place_results/pallas_call | solution.py:569
